TPU v7x, 128 devices: a whole 4x4x4 slice. The times are simulated.
128 devices in a mesh: ty: 16 (over x, y), tx: 8 (over z, core).
Axes of the slice: x: 4, y: 4, z: 4, core: 2. Of those that a mesh axis runs over, the one named last changes fastest.
Arguments:
- raw_bricks: bfloat16 [128, 3, 4, 4096], P(('ty', 'tx')), may hold values from -6 to 6
- stretch_reader: int32 [128], replicated, may hold values from 0 to 127, as said below
- fine_open: bfloat16 [3, 3, 3, 32, 1], replicated, may hold values from -1.75 to 1.75
- fine_second: bfloat16 [3, 3, 3, 32, 32], replicated, may hold values from -0.3125 to 0.3125
- middle_open: bfloat16 [3, 3, 3, 64, 32], replicated, may hold values from -0.3125 to 0.3125
- middle_second: bfloat16 [3, 3, 3, 64, 64], replicated, may hold values from -0.21875 to 0.21875
- coarse_open: bfloat16 [3, 3, 3, 64, 64], replicated, may hold values from -0.21875 to 0.21875
- coarse_second: bfloat16 [3, 3, 3, 64, 64], replicated, may hold values from -0.21875 to 0.21875
- middle_merge: bfloat16 [3, 3, 3, 64, 128], replicated, may hold values from -0.15625 to 0.15625
- middle_final: bfloat16 [3, 3, 3, 64, 64], replicated, may hold values from -0.21875 to 0.21875
- fine_merge: bfloat16 [3, 3, 3, 32, 96], replicated, may hold values from -0.15625 to 0.15625
- fine_final: bfloat16 [3, 3, 3, 32, 32], replicated, may hold values from -0.3125 to 0.3125
- affinity_head: bfloat16 [3, 32], replicated, may hold values from -1 to 1
Outputs:
- affinity_logits: float32 [3, 32, 256, 256], P(None, None, 'ty', 'tx')
Inputs may be any that keep to these rules, and one draw needn't show every extreme that they name: `stretch_reader`: stretch cy * 8 + cx is read by a device cy * 8 + j of the same row of tiles. In every row of tiles one or more devices read exactly 3 stretches, and every other device of the row reads one stretch or none.
All inputs are finite; a program needn't handle non-finite values.
Results may differ from a plain program's by a relative error of at most 0.04.
Values may be sent and summed in bfloat16 or wider, within the bound.
A program may use at most 128 MiB of HBM per device.

v0:
```python
import jax
import jax.numpy as jnp
from jax import lax
from jax.experimental import pallas as pl
from jax.experimental.pallas import tpu as pltpu
from jax.sharding import PartitionSpec as P

TILE_Y = 16
TILE_X = 32
DEPTH = 32
BF16 = jnp.bfloat16
F32 = jnp.float32
MIB = 1 << 20


def iota(shape, dim):
    return lax.broadcasted_iota(jnp.int32, shape, dim)


def lane_block(shape, width):
    return lax.shift_right_logical(iota(shape, len(shape) - 1), width.bit_length() - 1)


def spread_blocks(w_ref, out_chans, out_dim=0):
    eye = (iota((out_chans, 128), 0) == iota((out_chans, 128), 1) % out_chans).astype(BF16)
    return [
        lax.dot_general(w_ref[t], eye, (((out_dim,), (0,)), ((), ())), preferred_element_type=F32)
        for t in range(27)
    ]


def tap(a, b, e):
    if 0 <= a <= 2 and 0 <= b <= 2 and 0 <= e <= 2:
        return 9 * a + 3 * b + e
    return None


def masked_sum(blocks, taps, width):
    shape = blocks[0].shape
    lanes = lane_block(shape, width)
    tile = jnp.zeros(shape, F32)
    for place, index in enumerate(taps):
        if index is not None:
            tile = jnp.where(lanes == place, blocks[index], tile)
    return tile


def build_fine(blocks, out_ref):
    for y in range(4):
        for j in range(2):
            for half in range(2):
                for px_in in range(2):
                    for slot in range(2):
                        z = (1 + slot) if half == 0 else (3, 0)[slot]
                        row = (y * 2 + j) * 256 + half * 128 + px_in * 64 + slot * 32
                        for py in range(2):
                            taps = [
                                tap(z - pz, y - py, 2 * j + px_in - px)
                                for px in range(2)
                                for pz in range(2)
                            ]
                            out_ref[row : row + 32, py * 128 : (py + 1) * 128] = masked_sum(
                                blocks, taps, 32
                            ).astype(BF16)


def build_middle(blocks, out_ref):
    for y in range(4):
        for j in range(2):
            for slot, dz in enumerate((1, 0, 2)):
                for px_in in range(2):
                    row = (y * 2 + j) * 384 + slot * 128 + px_in * 64
                    for py in range(2):
                        taps = [tap(dz, y - py, 2 * j + px_in - px) for px in range(2)]
                        out_ref[row : row + 64, py * 128 : (py + 1) * 128] = masked_sum(
                            blocks, taps, 64
                        ).astype(BF16)


def build_middle_open(blocks, out_ref):
    for y in range(4):
        for j in range(2):
            for px_in in range(2):
                for slot, dz in enumerate((1, 0, 2, 9)):
                    row = (y * 2 + j) * 256 + px_in * 128 + slot * 32
                    for py in range(2):
                        taps = [tap(dz, y - py, 2 * j + px_in - px) for px in range(2)]
                        out_ref[row : row + 32, py * 128 : (py + 1) * 128] = masked_sum(
                            blocks, taps, 64
                        ).astype(BF16)


def build_up(zcombined, out_ref, row0):
    shape = (64, 128)
    odd = lane_block(shape, 64) == 1
    for slot in range(4):
        for xc in range(2):
            rows = None
            if slot < 3:
                rows = []
                for dy in range(3):
                    t = zcombined[slot][dy]
                    if xc == 0:
                        rows.append(jnp.where(odd, t[0], t[0] + t[1]))
                    else:
                        rows.append(jnp.where(odd, t[1] + t[2], t[2]))
            for yc in range(2):
                row = row0 + (yc * 2 + xc) * 256 + slot * 64
                for py in range(2):
                    if rows is None:
                        tile = jnp.zeros(shape, F32)
                    elif (py, yc) == (0, 0):
                        tile = rows[0] + rows[1]
                    elif (py, yc) == (0, 1):
                        tile = rows[2]
                    elif (py, yc) == (1, 0):
                        tile = rows[0]
                    else:
                        tile = rows[1] + rows[2]
                    out_ref[row : row + 64, py * 128 : (py + 1) * 128] = tile.astype(BF16)


def build_open(w_ref, base_ref, out_ref):
    base_ref[...] = jnp.zeros_like(base_ref)
    eye = (iota((32, 128), 0) == iota((32, 128), 1) % 32).astype(BF16)
    rows = []
    for t in range(9):
        three = jnp.dot(w_ref[t], eye, preferred_element_type=F32)
        rows += [three[dx : dx + 1] for dx in range(3)]
    for dy in range(3):
        for z in range(6):
            for x in range(4):
                row = 40 + z // 3 * 128 + z % 3 * 40 + x
                for half in range(2):
                    taps = []
                    for px in range(2):
                        for p in range(2):
                            z_out = p if half == 0 else (2, -1)[p]
                            taps.append(tap(z - 1 - z_out, dy, x - px))
                    base_ref[dy, row : row + 1, 128 * half : 128 * half + 128] = masked_sum(
                        rows, taps, 32
                    )
    for xp in range(17):
        for dy in range(3):
            out_ref[xp, 256 * dy : 256 * dy + 256] = base_ref[
                dy, 40 - 2 * xp : 296 - 2 * xp
            ].astype(BF16)


def build_middle_merge(w_ref, out_ref):
    both = spread_blocks(w_ref, 64)
    build_middle([block[64:128] for block in both], out_ref)
    up = [block[:64] for block in both]
    grid = [[[up[9 * dz + 3 * dy + dx] for dx in range(3)] for dy in range(3)] for dz in (1, 0, 2)]
    build_up(grid, out_ref, 3072)


def build_fine_merge(w_ref, out_ref):
    both = spread_blocks(w_ref, 32)
    build_fine([block[64:96] for block in both], out_ref)
    up = [block[:64] for block in both]
    odd_z = lane_block((64, 128), 32) % 2 == 1

    def zmix(slot, dy, dx):
        w0, w1, w2 = (up[9 * a + 3 * dy + dx] for a in range(3))
        if slot == 0:
            return jnp.where(odd_z, w0 + w1, w1 + w2)
        if slot == 1:
            return jnp.where(odd_z, 0.0, w0)
        return jnp.where(odd_z, w2, 0.0)

    grid = [[[zmix(slot, dy, dx) for dx in range(3)] for dy in range(3)] for slot in range(3)]
    build_up(grid, out_ref, 2048)


def build_head(head_ref, out_ref):
    column = iota((256, 32), 0) % 128 // 32
    picked = jnp.zeros((256, 32), F32)
    for c in range(3):
        picked = jnp.where(column == c, head_ref[c : c + 1, :].astype(F32), picked)
    eye = (iota((256, 32), 0) % 32 == iota((256, 32), 1)).astype(BF16)
    full = lax.dot_general(
        eye, picked.astype(BF16), (((1,), (1,)), ((), ())), preferred_element_type=F32
    )
    row, col = iota((256, 256), 0), iota((256, 256), 1)
    fits = (row // 64 % 2 == col // 128) & (row // 32 % 2 == col // 16 % 2)
    fits = fits & (row // 128 == col % 16) & (col % 128 < 96)
    base = jnp.where(fits, full, 0.0)
    for yg in range(8):
        for px in range(2):
            part = base[:, 128 * px : 128 * px + 128]
            out_ref[256 * yg : 256 * yg + 256, 128 * px : 128 * px + 128] = pltpu.roll(
                part, 2 * yg, 1
            ).astype(BF16)


class Masks:
    def __init__(self):
        row, lane = iota((16, 128), 0), iota((16, 128), 1)

        def factor(where):
            return jnp.where(where, 1.0, 0.0).astype(F32)

        first, last = row > 0, row < 15
        odd = (lane & 32) != 0
        self.below, self.above = factor(first), factor(last)
        self.ends_below, self.ends_above = factor(odd & first), factor(~odd & last)
        self.low, self.high_below = factor(lane < 64), factor((lane >= 64) & first)
        self.px = [factor(lane < 64), factor(lane >= 64)]
        self.coarse_z = factor(row < 8)
        block = lane >> 5
        self.block = [factor(block == 0), factor((block == 1) & first), factor((block == 2) & last)]


def scaled(x, factor):
    return as_rows(as_blocks(x) * factor[None])


def row_below(x):
    return pltpu.roll(x, 1, 0)


def row_above(x):
    return pltpu.roll(x, x.shape[0] - 1, 0)


def as_rows(x):
    return x.reshape(x.shape[0] * 16, x.shape[2])


def as_blocks(x):
    return x.reshape(x.shape[0] // 16, 16, x.shape[1])


def up_window(src, yg, shift, groups):
    y, x = yg + shift, shift
    return [as_rows(src[y + yc, x + xc : x + xc + groups]) for yc in range(2) for xc in range(2)]


def window(src, yg, groups, up=None):
    pieces = [as_rows(src[2 * yg + y, j : j + groups]) for y in range(4) for j in range(2)]
    if up is not None:
        pieces += up_window(up, yg, 0, groups)
    return jnp.concatenate(pieces, axis=1)


def conv(src, w_ref, yg, groups):
    lhs = window(src, yg, groups)
    return jnp.dot(lhs, w_ref[...], preferred_element_type=F32)


def conv_lines(src, w_ref, counts, groups, body, up=None):
    first, rows = 0, groups * 16
    for count in counts:
        lines = range(first, first + count)
        lhs = jnp.concatenate([window(src, yg, groups, up) for yg in lines], axis=0)
        acc = jnp.dot(lhs, w_ref[...], preferred_element_type=F32)
        for i, yg in enumerate(lines):
            body(yg, acc[i * rows : (i + 1) * rows])
        first += count


def store_fine(ref, y, tile, m):
    ends = scaled(row_below(tile), m.ends_below) + scaled(row_above(tile), m.ends_above)
    ref[y, :, :, 0:128] = as_blocks(tile.astype(BF16))
    ref[y, :, :, 128:256] = as_blocks(ends.astype(BF16))


def store_middle(ref, y, tile, m):
    ref[y, :, :, 0:128] = as_blocks(tile.astype(BF16))
    ref[y, :, :, 128:256] = as_blocks(scaled(row_below(tile), m.below).astype(BF16))
    ref[y, :, :, 256:384] = as_blocks(scaled(row_above(tile), m.above).astype(BF16))


def store_single(ref, y, tile, m):
    below, above = row_below(tile), scaled(row_above(tile), m.above)
    near = [
        scaled(tile, m.low) + scaled(pltpu.roll(below, 64, 1), m.high_below),
        scaled(pltpu.roll(tile, 64, 1), m.low) + scaled(below, m.high_below),
    ]
    far = [above, pltpu.roll(above, 64, 1)]
    for px in range(2):
        a, b = as_blocks(near[px].astype(BF16)), as_blocks(far[px].astype(BF16))
        for xg in range(tile.shape[0] // 16):
            ref[y, 2 * xg + px, :, 0:128] = a[xg]
            ref[y, 2 * xg + px, :, 128:256] = b[xg]


def clear_outside(ref, lines, places, ty, tx, m, split=False):
    count = ref.shape[1]
    parts = ref.shape[3] // 128

    def halve(place, px):
        factor = jnp.concatenate([m.px[px]] * parts, axis=1).astype(BF16)
        ref[:, place] = ref[:, place] * factor[None]

    @pl.when(ty == 0)
    def _():
        ref[0:lines] = jnp.zeros((lines,) + ref.shape[1:], BF16)

    @pl.when(ty == 15)
    def _():
        ref[ref.shape[0] - lines :] = jnp.zeros((lines,) + ref.shape[1:], BF16)

    @pl.when(tx == 0)
    def _():
        if places:
            ref[:, 0:places] = jnp.zeros((ref.shape[0], places) + ref.shape[2:], BF16)
        if split:
            halve(places, 1)

    @pl.when(tx == 7)
    def _():
        if places:
            ref[:, count - places :] = jnp.zeros((ref.shape[0], places) + ref.shape[2:], BF16)
        if split:
            halve(count - 1 - places, 0)


def loop(count, body, unroll=1):
    def step(i, carry):
        body(i)
        return carry

    lax.fori_loop(0, count, step, 0, unroll=unroll)


AROUND = [(-1, 0), (1, 0), (-1, -1), (-1, 1), (1, -1), (1, 1), (0, -1), (0, 1)]
ALONG_TY, ALONG_TX = range(6), range(6, 8)


def span(step, core, width):
    if step == 0:
        return width, width, core
    if step > 0:
        return core, 0, width
    return width, core + width, width


def exchange(ref, widths, send_sems, recv_sems, ty, tx, directions=range(8)):
    copies = []
    for i in directions:
        dy, dx = AROUND[i]
        sy, ly, ny = span(dy, ref.shape[0] - 2 * widths[0], widths[0])
        sx, lx, nx = span(dx, ref.shape[1] - 2 * widths[1], widths[1])
        copy = pltpu.make_async_remote_copy(
            src_ref=ref.at[pl.ds(sy, ny), pl.ds(sx, nx)],
            dst_ref=ref.at[pl.ds(ly, ny), pl.ds(lx, nx)],
            send_sem=send_sems.at[i],
            recv_sem=recv_sems.at[i],
            device_id=((ty + dy + 16) % 16, (tx + dx + 8) % 8),
            device_id_type=pl.DeviceIdType.MESH,
        )
        sends, receives = neighbour(dy, dx, ty, tx), neighbour(-dy, -dx, ty, tx)
        pl.when(sends)(copy.start)
        copies.append((copy, sends, receives))
    return copies


def neighbour(dy, dx, ty, tx):
    there = [tx >= 0]
    if dy:
        there.append(ty < 15 if dy > 0 else ty > 0)
    if dx:
        there.append(tx < 7 if dx > 0 else tx > 0)
    return there[-1] if len(there) < 3 else there[1] & there[2]


def finish(copies):
    for copy, sends, receives in copies:
        pl.when(receives)(copy.wait_recv)
    for copy, sends, receives in copies:
        pl.when(sends)(copy.wait_send)


def whole_kernel(
    readers, raw, head, fo, fs, mo, ms, co, cs, mm, mf, fm, ff,
    out,
    r_fs, r_mo, r_ms, r_co, r_cs, r_mm, r_mf, r_fm, r_ff,
    w_fo, w_fs, w_mo, w_ms, w_co, w_cs, w_mm, w_mf, w_fm, w_ff, w_head,
    outgoing, arrived, held,
    base_ref, z_ref, a_ref,
    quads, skip, in_ref, b_ref, s_ref,
    coarse, middle, ci_ref, co_ref, s2_ref, u1_ref, mi_ref, mm_ref, u2_ref, fi_ref, fm_ref,
    part_ref, last_ref, first_ref, second_ref, turn_ref, bricks_ref,
    load_sems, row_send, row_recv, near_send, near_recv,
    quad_send, quad_recv, skip_send, skip_recv, coarse_send, coarse_recv, middle_send, middle_recv,
):
    ty, tx = lax.axis_index("ty"), lax.axis_index("tx")
    m = Masks()
    mesh_id = pl.DeviceIdType.MESH
    loads = [
        pltpu.make_async_copy(source, target, load_sems.at[i])
        for i, (source, target) in enumerate(
            zip((fs, mo, ms, co, cs, mm, mf, fm, ff), (r_fs, r_mo, r_ms, r_co, r_cs, r_mm, r_mf, r_fm, r_ff))
        )
    ]
    for load in loads:
        load.start()

    barrier = pltpu.get_barrier_semaphore()
    greeted = [(ty, (tx + d) % 8) for d in range(1, 8)]
    greeted += [((ty + dy + 16) % 16, (tx + dx + 8) % 8) for dy in (-1, 1) for dx in (-1, 0, 1)]
    for device in greeted:
        pl.semaphore_signal(barrier, inc=1, device_id=device, device_id_type=mesh_id)
    for slot in range(3):
        for z in range(32):
            bricks_ref[slot, pl.ds(z, 4, stride=32), :] = raw[
                slot, :, 128 * z : 128 * z + 128
            ].astype(F32)

    pl.semaphore_wait(barrier, len(greeted))

    reader = [readers[ty * 8 + c] for c in range(8)]
    for c in range(8):
        rank = 0
        for earlier in range(c):
            rank += (reader[earlier] == reader[c]).astype(jnp.int32)
        outgoing[c] = bricks_ref[jnp.minimum(rank, 2)].astype(BF16).reshape(4, 32, 128)
    copies = []
    for d in range(1, 8):
        peer = (tx + d) % 8
        copy = pltpu.make_async_remote_copy(
            src_ref=outgoing.at[peer],
            dst_ref=arrived.at[tx],
            send_sem=row_send.at[d],
            recv_sem=row_recv.at[d],
            device_id=(ty, peer),
            device_id_type=mesh_id,
        )
        copy.start()
        copies.append(copy)
    arrived[tx] = outgoing[tx]
    build_open(fo, base_ref, w_fo)
    loads[0].wait()
    build_fine(spread_blocks(r_fs, 32), w_fs)
    for copy in copies:
        copy.wait()
    own = readers[ty * 8 + tx] % 8
    held[1, 1] = arrived[own]
    copies = []
    for i, (dy, dx) in enumerate([(0, 1), (1, 0), (1, 1)]):
        copy = pltpu.make_async_remote_copy(
            src_ref=held.at[1, 1],
            dst_ref=held.at[1 - dy, 1 - dx],
            send_sem=near_send.at[i],
            recv_sem=near_recv.at[i],
            device_id=((ty + dy) % 16, (tx + dx) % 8),
            device_id_type=mesh_id,
        )
        copy.start()
        copies.append(copy)
    loads[1].wait()
    build_middle_open(spread_blocks(r_mo, 64, 1), w_mo)
    loads[2].wait()
    build_middle(spread_blocks(r_ms, 64), w_ms)
    loads[3].wait()
    build_middle(spread_blocks(r_co, 64), w_co)
    for copy in copies:
        copy.wait()

    z_ref[:, 0:8] = jnp.zeros((20, 8, 128), F32)
    z_ref[:, 32:40] = jnp.zeros((20, 8, 128), F32)
    lane = iota((32, 128), 1)
    lines = []
    for br in range(4):
        bricks = []
        for bc in range(4):
            brick = held[br // 2, bc // 2, br % 2 * 2 + bc % 2].astype(F32)
            ok = True
            if br == 0:
                ok = ty > 0
            if br == 3:
                ok = ty < 15
            if bc == 0:
                ok = (tx > 0) & ok
            if bc == 3:
                ok = (tx < 7) & ok
            if ok is not True:
                brick = jnp.where(ok, brick, 0.0)
            bricks.append(brick)
        for r in ((6, 7), range(8), range(8), (0, 1))[br]:
            y = 8 * br + r - 6
            line = jnp.where(lane < 36, pltpu.roll(bricks[3], (34 - 16 * r) % 128, 1), 0.0)
            line = jnp.where(lane < 34, pltpu.roll(bricks[2], (18 - 16 * r) % 128, 1), line)
            line = jnp.where(lane < 18, pltpu.roll(bricks[1], (2 - 16 * r) % 128, 1), line)
            line = jnp.where(lane < 2, pltpu.roll(bricks[0], (-14 - 16 * r) % 128, 1), line)
            z_ref[y, 4:36, :] = line
            parts = [z_ref[y, pl.ds(2 + z, 16, stride=2), :] for z in range(6)]
            for t in range(2):
                tile = parts[3 * t]
                for i in (1, 2):
                    tile = tile + pltpu.roll(parts[3 * t + i], 40 * i, 1)
                parts[t] = tile
            lines.append(jnp.concatenate(parts[:2], axis=1).astype(BF16))
    lhs = jnp.concatenate(
        [jnp.concatenate(lines[dy : dy + 18], axis=0) for dy in range(3)], axis=1
    )
    ends = m.ends_below + m.ends_above
    for xp in range(17):
        acc = jnp.maximum(jnp.dot(lhs, w_fo[xp], preferred_element_type=F32), 0.0)
        a_ref[:, xp, :, 0:128] = as_blocks(acc[:, :128].astype(BF16))
        a_ref[:, xp, :, 128:256] = as_blocks(scaled(acc[:, 128:], ends).astype(BF16))
    clear_outside(a_ref, 1, 0, ty, tx, m, split=True)
    quad_lane = lane_block((4, 16, 128), 32)

    def second(yg):
        acc = jnp.maximum(conv(a_ref, w_fs, yg, 16), 0.0)
        skip[2 + 2 * yg, 1:17] = as_blocks(acc[:, :128].astype(BF16))
        skip[3 + 2 * yg, 1:17] = as_blocks(acc[:, 128:].astype(BF16))
        top = jnp.maximum(acc[:, :128], acc[:, 128:])
        top = jnp.maximum(top, pltpu.roll(top, 64, 1))
        top = jnp.maximum(top, pltpu.roll(top, 32, 1)).reshape(4, 4, 16, 128)
        quad = top[:, 0]
        for q in range(1, 4):
            quad = jnp.where(quad_lane == q, top[:, q], quad)
        quads[2 + yg, 1:5] = quad.astype(BF16)

    for yg in (0, 1, 6, 7):
        second(yg)
    copies = exchange(quads, (2, 1), quad_send, quad_recv, ty, tx, ALONG_TY)
    for yg in range(2, 6):
        second(yg)
    copies += exchange(quads, (2, 1), quad_send, quad_recv, ty, tx, ALONG_TX)
    skip_copies = exchange(skip, (2, 1), skip_send, skip_recv, ty, tx)
    loads[4].wait()
    build_middle(spread_blocks(r_cs, 64), w_cs)
    loads[5].wait()
    build_middle_merge(r_mm, w_mm)
    loads[6].wait()
    build_middle(spread_blocks(r_mf, 64), w_mf)
    loads[7].wait()
    build_fine_merge(r_fm, w_fm)
    loads[8].wait()
    build_fine(spread_blocks(r_ff, 32), w_ff)
    build_head(head, w_head)
    finish(copies)

    clear_outside(quads, 2, 1, ty, tx, m)

    def spread(y):
        c = as_rows(quads[y]).astype(F32)
        below, above = row_below(c), row_above(c)
        for q in range(4):
            tile = scaled(pltpu.roll(c, (-32 * q) % 128, 1), m.block[0])
            tile = tile + scaled(pltpu.roll(below, (32 - 32 * q) % 128, 1), m.block[1])
            tile = tile + scaled(pltpu.roll(above, (64 - 32 * q) % 128, 1), m.block[2])
            blocks = as_blocks(tile.astype(BF16))
            lane = 128 * (q % 2)
            for quad in range(6):
                place = 2 * quad - 1 + q // 2
                if 0 <= place < 10:
                    in_ref[y, place, :, lane : lane + 128] = blocks[quad]

    loop(12, spread, 3)

    def middle_open(yg, acc):
        for py in range(2):
            tile = jnp.maximum(acc[:, 128 * py : 128 * py + 128], 0.0)
            store_middle(b_ref, 2 * yg + py, tile, m)

    conv_lines(in_ref, w_mo, (2, 3), 9, middle_open)
    clear_outside(b_ref, 1, 0, ty, tx, m, split=True)
    low = lane_block((4, 8, 128), 64) == 0

    def middle_second(yg, acc):
        acc = jnp.maximum(acc, 0.0)
        middle[4 + 2 * yg, 2:10] = as_blocks(acc[:, :128].astype(BF16))
        middle[5 + 2 * yg, 2:10] = as_blocks(acc[:, 128:].astype(BF16))
        top = jnp.maximum(acc[:, :128], acc[:, 128:])
        top = jnp.maximum(top, pltpu.roll(top, 64, 1))
        s_ref[yg] = jnp.maximum(top, row_above(top))
        some = s_ref[yg, pl.ds(0, 64, stride=2), :].reshape(4, 2, 8, 128)
        pair = jnp.where(low, some[:, 0], some[:, 1])
        coarse[4 + yg, 1:3] = pair.reshape(2, 16, 128).astype(BF16)

    conv_lines(b_ref, w_ms, (2, 2), 8, middle_second)
    copies = exchange(coarse, (4, 1), coarse_send, coarse_recv, ty, tx)
    middle_copies = exchange(middle, (4, 2), middle_send, middle_recv, ty, tx)

    finish(skip_copies)
    clear_outside(skip, 2, 1, ty, tx, m)

    def fine_in(y):
        x = as_rows(skip[y]).astype(F32)
        store_fine(fi_ref, y, x, m)

    loop(20, fine_in, 2)
    for yg in range(9):
        part_ref[yg] = jnp.dot(
            window(fi_ref, yg, 17), w_fm[0:2048], preferred_element_type=F32
        )
    finish(copies)

    clear_outside(coarse, 4, 1, ty, tx, m)

    def coarse_in(y):
        x = coarse[y].astype(F32).reshape(8, 8, 128)
        x = as_rows(jnp.concatenate([x, jnp.zeros_like(x)], axis=1))
        store_middle(ci_ref, y, x, m)

    loop(12, coarse_in)

    def coarse_open(yg, acc):
        for py in range(2):
            tile = jnp.maximum(acc[:, 128 * py : 128 * py + 128], 0.0)
            tile = scaled(tile, m.coarse_z)
            store_middle(co_ref, 2 * yg + py, tile, m)

    conv_lines(ci_ref, w_co, (2, 3), 7, coarse_open)
    clear_outside(co_ref, 3, 1, ty, tx, m, split=True)

    def coarse_second(yg, acc):
        for py in range(2):
            tile = jnp.maximum(acc[:, 128 * py : 128 * py + 128], 0.0)
            half = tile.reshape(6, 16, 128)[:, :8].reshape(48, 128)
            s2_ref[2 * yg + py, pl.ds(0, 48, stride=2), :] = half
            s2_ref[2 * yg + py, pl.ds(1, 48, stride=2), :] = half
            store_single(u1_ref, 2 * yg + py, s2_ref[2 * yg + py], m)

    conv_lines(co_ref, w_cs, (2, 2), 6, coarse_second)
    clear_outside(u1_ref, 2, 2, ty, tx, m)
    finish(middle_copies)
    clear_outside(middle, 4, 2, ty, tx, m)

    def middle_in(y):
        x = as_rows(middle[y]).astype(F32)
        store_middle(mi_ref, y, x, m)

    loop(16, middle_in)

    def middle_merge(yg, acc):
        for py in range(2):
            tile = jnp.maximum(acc[:, 128 * py : 128 * py + 128], 0.0)
            store_middle(mm_ref, 2 * yg + py, tile, m)

    conv_lines(mi_ref, w_mm, (2, 2, 3), 11, middle_merge, u1_ref)
    clear_outside(mm_ref, 3, 1, ty, tx, m, split=True)

    def middle_final(yg, acc):
        for py in range(2):
            tile = jnp.maximum(acc[:, 128 * py : 128 * py + 128], 0.0)
            store_single(u2_ref, 2 * yg + py, tile, m)

    conv_lines(mm_ref, w_mf, (2, 2, 2), 10, middle_final)
    clear_outside(u2_ref, 2, 2, ty, tx, m)


    def fine_merge(yg):
        acc = part_ref[yg] + jnp.dot(
            jnp.concatenate(up_window(u2_ref, yg, 1, 17), axis=1),
            w_fm[2048:3072],
            preferred_element_type=F32,
        )
        for py in range(2):
            tile = jnp.maximum(acc[:, 128 * py : 128 * py + 128], 0.0)
            store_fine(fm_ref, 2 * yg + py, tile, m)

    for yg in range(9):
        fine_merge(yg)
    clear_outside(fm_ref, 1, 0, ty, tx, m, split=True)

    def fine_final(yg):
        last_ref[yg] = jnp.maximum(conv(fm_ref, w_ff, yg, 16), 0.0).astype(BF16)

    for yg in range(8):
        fine_final(yg)
    logits = jnp.dot(
        jnp.concatenate([last_ref[yg] for yg in range(8)], axis=1),
        w_head[...],
        preferred_element_type=F32,
    )
    first_ref[...] = logits[:, :128]
    second_ref[...] = logits[:, 128:]

    def finished(k):
        turn_ref[k, pl.ds(0, 16, stride=2), :] = first_ref[pl.ds(k, 16, stride=16), :]
        turn_ref[k, pl.ds(1, 16, stride=2), :] = second_ref[pl.ds(k, 16, stride=16), :]
        turned = turn_ref[k].T
        for c in range(3):
            for pz in range(2):
                row = 32 * c + 16 * pz
                out[c, 2 * k + pz] = turned[row : row + 16]

    for k in range(16):
        finished(k)


def per_device(
    raw_bricks,
    stretch_reader,
    fine_open,
    fine_second,
    middle_open,
    middle_second,
    coarse_open,
    coarse_second,
    middle_merge,
    middle_final,
    fine_merge,
    fine_final,
    affinity_head,
):
    def flat(w):
        return w.reshape(27, w.shape[3], w.shape[4])

    weights = [
        flat(fine_second),
        flat(middle_open.transpose(0, 1, 2, 4, 3)),
        flat(middle_second),
        flat(coarse_open),
        flat(coarse_second),
        flat(middle_merge),
        flat(middle_final),
        flat(fine_merge),
        flat(fine_final),
    ]
    opening = fine_open.transpose(0, 1, 4, 2, 3).reshape(9, 3, 32)
    vmem = pl.BlockSpec(memory_space=pltpu.VMEM)
    smem = pl.BlockSpec(memory_space=pltpu.SMEM)
    hbm = pl.BlockSpec(memory_space=pl.ANY)
    dma = pltpu.SemaphoreType.DMA

    def half(*shape):
        return pltpu.VMEM(shape, BF16)

    def full(*shape):
        return pltpu.VMEM(shape, F32)

    return pl.pallas_call(
        whole_kernel,
        out_shape=jax.ShapeDtypeStruct((3, DEPTH, TILE_Y, TILE_X), F32),
        in_specs=[smem] + [vmem] * 3 + [hbm] * 9,
        out_specs=vmem,
        scratch_shapes=[half(*w.shape) for w in weights]
        + [half(17, 768, 256)]
        + [half(size, 256) for size in (2048, 2048, 3072, 3072, 3072, 4096, 3072, 3072, 2048, 2048)]
        + [
            half(8, 4, 32, 128),
            half(8, 4, 32, 128),
            half(2, 2, 4, 32, 128),
            full(3, 296, 256),
            full(20, 40, 128),
            half(18, 17, 16, 256),
            half(12, 6, 16, 128),
            half(20, 18, 16, 128),
            half(12, 10, 16, 256),
            half(10, 9, 16, 384),
            full(4, 128, 128),
            half(12, 4, 16, 128),
            half(16, 12, 16, 128),
            half(12, 8, 16, 384),
            half(10, 7, 16, 384),
            full(8, 96, 128),
            half(8, 12, 16, 256),
            half(16, 12, 16, 384),
            half(14, 11, 16, 384),
            half(12, 20, 16, 256),
            half(20, 18, 16, 256),
            half(18, 17, 16, 256),
            full(9, 272, 256),
            half(8, 256, 256),
            full(256, 128),
            full(256, 128),
            full(16, 32, 128),
            full(3, 128, 128),
            dma((9,)),
            dma((8,)),
            dma((8,)),
            dma((3,)),
            dma((3,)),
        ]
        + [dma((8,))] * 8,
        name="whole",
        compiler_params=pltpu.CompilerParams(
            vmem_limit_bytes=58 * MIB, collective_id=0, has_side_effects=True
        ),
        cost_estimate=pl.CostEstimate(flops=10**10, bytes_accessed=10**7, transcendentals=0),
    )(stretch_reader, raw_bricks[0], affinity_head, opening, *weights)


def solution(mesh):
    placed = (P(("ty", "tx"), None, None, None),) + (P(),) * 12
    return jax.shard_map(
        per_device, mesh=mesh, in_specs=placed, out_specs=P(None, None, "ty", "tx"), check_vma=False
    )
```

profile of v0, /device:TPU:1, one launch (start us, length us, event | category | flops | bytes accessed | tf_op | source)
XLA Modules:
  0.0 53.4 jit_solution(9191908351603475609)
XLA Ops:
  0.0 51.3 %whole.1 = f32[3,32,16,32]{3,2,1,0:T(8,128)} custom-call(s32[128]{0:T(128)} %readers.1, bf16[3,4,4096]{2,1,0:T(4,128)(2,1)} %bitcast.22, bf16[3,32]{1,0:T(4,128)(2,1)} %head.1, bf16[9,3,32]{2,1,0:T(4,128)(2,1)} %bitcast.23, bf16[27,32,32]{2,1,0:T(8,128)(2,1)} %bitcast.18, bf16[27,32,64]{2,1,0:T(8,128)(2,1)} %bitcast.19, bf16[27,64,64]{2,1,0:T(8,128)(2,1)} %bitcast.13, ...), custom_call_target="tpu_custom_call" | custom-call | flops 10000000000 | bytes 10000000 | tf_op jit(solution)/shard_map/whole/pallas_call | solution.py:730
  51.3 2.1 %copy.15 = f32[3,32,16,32]{3,2,1,0:T(8,128)} copy(f32[3,32,16,32]{3,2,1,0:T(8,128)} %whole.1) | data formatting | bytes 393216
where the time goes:
time: 53.5 us; the launch traced here: 53.4 us
  Pallas kernels  51.3 us (96%)
  local copies, waits for them, and re-layouts  2.06 us (4%)
    pallas_call x1, Pallas kernels, per_device(): pl.pallas_call(whole_kernel, out_shape=jax.ShapeDtypeStruct((3, DEPTH, TI...  51.3 us
    unnamed x1, local copies, waits for them, and re-layouts  2.06 us

commit v1 on v0

--- a/solution.py
+++ b/solution.py
@@ -249,9 +249,11 @@
     return jnp.dot(lhs, w_ref[...], preferred_element_type=F32)
 
 
-def conv_lines(src, w_ref, counts, groups, body, up=None):
+def conv_lines(src, w_ref, counts, groups, body, up=None, beside=None):
     first, rows = 0, groups * 16
-    for count in counts:
+    for number, count in enumerate(counts):
+        if beside is not None:
+            beside(number)
         lines = range(first, first + count)
         lhs = jnp.concatenate([window(src, yg, groups, up) for yg in lines], axis=0)
         acc = jnp.dot(lhs, w_ref[...], preferred_element_type=F32)
@@ -382,7 +384,7 @@
     base_ref, z_ref, a_ref,
     quads, skip, in_ref, b_ref, s_ref,
     coarse, middle, ci_ref, co_ref, s2_ref, u1_ref, mi_ref, mm_ref, u2_ref, fi_ref, fm_ref,
-    part_ref, last_ref, first_ref, second_ref, turn_ref, bricks_ref,
+    part_ref, last_ref, bricks_ref,
     load_sems, row_send, row_recv, near_send, near_recv,
     quad_send, quad_recv, skip_send, skip_recv, coarse_send, coarse_recv, middle_send, middle_recv,
 ):
@@ -552,14 +554,17 @@
                 if 0 <= place < 10:
                     in_ref[y, place, :, lane : lane + 128] = blocks[quad]
 
-    loop(12, spread, 3)
+    def spread_lines(number):
+        for y in (range(6), range(6, 12))[number]:
+            spread(y)
+
 
     def middle_open(yg, acc):
         for py in range(2):
             tile = jnp.maximum(acc[:, 128 * py : 128 * py + 128], 0.0)
             store_middle(b_ref, 2 * yg + py, tile, m)
 
-    conv_lines(in_ref, w_mo, (2, 3), 9, middle_open)
+    conv_lines(in_ref, w_mo, (2, 3), 9, middle_open, beside=spread_lines)
     clear_outside(b_ref, 1, 0, ty, tx, m, split=True)
     low = lane_block((4, 8, 128), 64) == 0
 
@@ -585,13 +590,18 @@
         x = as_rows(skip[y]).astype(F32)
         store_fine(fi_ref, y, x, m)
 
-    loop(20, fine_in, 2)
-    for yg in range(9):
+    def fine_part(yg):
+        for y in range(4) if yg == 0 else (2 * yg + 2, 2 * yg + 3):
+            fine_in(y)
         part_ref[yg] = jnp.dot(
             window(fi_ref, yg, 17), w_fm[0:2048], preferred_element_type=F32
         )
+
+    for yg in range(4):
+        fine_part(yg)
     finish(copies)
-
+    finish(middle_copies)
+    clear_outside(middle, 4, 2, ty, tx, m)
     clear_outside(coarse, 4, 1, ty, tx, m)
 
     def coarse_in(y):
@@ -599,7 +609,20 @@
         x = as_rows(jnp.concatenate([x, jnp.zeros_like(x)], axis=1))
         store_middle(ci_ref, y, x, m)
 
-    loop(12, coarse_in)
+    def middle_in(y):
+        x = as_rows(middle[y]).astype(F32)
+        store_middle(mi_ref, y, x, m)
+
+    def beside_open(number):
+        for y in (range(6), range(6, 12))[number]:
+            coarse_in(y)
+        fine_part(4 + number)
+
+    def beside_second(number):
+        for y in (range(8), range(8, 16))[number]:
+            middle_in(y)
+        fine_part(6 + number)
+
 
     def coarse_open(yg, acc):
         for py in range(2):
@@ -607,7 +630,7 @@
             tile = scaled(tile, m.coarse_z)
             store_middle(co_ref, 2 * yg + py, tile, m)
 
-    conv_lines(ci_ref, w_co, (2, 3), 7, coarse_open)
+    conv_lines(ci_ref, w_co, (2, 3), 7, coarse_open, beside=beside_open)
     clear_outside(co_ref, 3, 1, ty, tx, m, split=True)
 
     def coarse_second(yg, acc):
@@ -618,16 +641,9 @@
             s2_ref[2 * yg + py, pl.ds(1, 48, stride=2), :] = half
             store_single(u1_ref, 2 * yg + py, s2_ref[2 * yg + py], m)
 
-    conv_lines(co_ref, w_cs, (2, 2), 6, coarse_second)
+    conv_lines(co_ref, w_cs, (2, 2), 6, coarse_second, beside=beside_second)
+    fine_part(8)
     clear_outside(u1_ref, 2, 2, ty, tx, m)
-    finish(middle_copies)
-    clear_outside(middle, 4, 2, ty, tx, m)
-
-    def middle_in(y):
-        x = as_rows(middle[y]).astype(F32)
-        store_middle(mi_ref, y, x, m)
-
-    loop(16, middle_in)
 
     def middle_merge(yg, acc):
         for py in range(2):
@@ -670,20 +686,19 @@
         w_head[...],
         preferred_element_type=F32,
     )
-    first_ref[...] = logits[:, :128]
-    second_ref[...] = logits[:, 128:]
-
-    def finished(k):
-        turn_ref[k, pl.ds(0, 16, stride=2), :] = first_ref[pl.ds(k, 16, stride=16), :]
-        turn_ref[k, pl.ds(1, 16, stride=2), :] = second_ref[pl.ds(k, 16, stride=16), :]
+    out[0] = logits[:, :128]
+    out[1] = logits[:, 128:]
+
+
+def finish_kernel(logits, out, turn_ref):
+    for k in range(16):
+        turn_ref[k, pl.ds(0, 16, stride=2), :] = logits[0, pl.ds(k, 16, stride=16), :]
+        turn_ref[k, pl.ds(1, 16, stride=2), :] = logits[1, pl.ds(k, 16, stride=16), :]
         turned = turn_ref[k].T
         for c in range(3):
             for pz in range(2):
                 row = 32 * c + 16 * pz
                 out[c, 2 * k + pz] = turned[row : row + 16]
-
-    for k in range(16):
-        finished(k)
 
 
 def per_device(
@@ -727,9 +742,9 @@
     def full(*shape):
         return pltpu.VMEM(shape, F32)
 
-    return pl.pallas_call(
+    logits = pl.pallas_call(
         whole_kernel,
-        out_shape=jax.ShapeDtypeStruct((3, DEPTH, TILE_Y, TILE_X), F32),
+        out_shape=jax.ShapeDtypeStruct((2, 256, 128), F32),
         in_specs=[smem] + [vmem] * 3 + [hbm] * 9,
         out_specs=vmem,
         scratch_shapes=[half(*w.shape) for w in weights]
@@ -760,9 +775,6 @@
             half(18, 17, 16, 256),
             full(9, 272, 256),
             half(8, 256, 256),
-            full(256, 128),
-            full(256, 128),
-            full(16, 32, 128),
             full(3, 128, 128),
             dma((9,)),
             dma((8,)),
@@ -777,6 +789,15 @@
         ),
         cost_estimate=pl.CostEstimate(flops=10**10, bytes_accessed=10**7, transcendentals=0),
     )(stretch_reader, raw_bricks[0], affinity_head, opening, *weights)
+    return pl.pallas_call(
+        finish_kernel,
+        out_shape=jax.ShapeDtypeStruct((3, DEPTH, TILE_Y, TILE_X), F32),
+        in_specs=[vmem],
+        out_specs=vmem,
+        scratch_shapes=[full(16, 32, 128)],
+        name="finish",
+        compiler_params=pltpu.CompilerParams(vmem_limit_bytes=4 * MIB),
+    )(logits)
 
 
 def solution(mesh):

time: 53.5 us -> 56.5 us (1.056)
  Pallas kernels: 51.3 us -> 55.4 us
  local copies, waits for them, and re-layouts: 2.06 us -> 0.94 us
    pallas_call x1 -> x2, Pallas kernels: 51.3 us -> 55.4 us  [the longest x1 54.2 us: per_device(): pl.pallas_call(whole_kernel, out_shape=jax.ShapeDtypeStruct((2, 256, 128)...]
    unnamed x1 -> x2, local copies, waits for them, and re-layouts: 2.06 us -> 0.94 us
where the time goes in v1:
time: 56.5 us; the launch traced here: 56.3 us
  Pallas kernels  55.4 us (98%)
  local copies, waits for them, and re-layouts  0.94 us (2%)
    pallas_call x1, Pallas kernels, per_device(): pl.pallas_call(whole_kernel, out_shape=jax.ShapeDtypeStruct((2, 256, 128)...  54.2 us
    pallas_call x1, Pallas kernels, per_device(): pl.pallas_call(finish_kernel, out_shape=jax.ShapeDtypeStruct((3, DEPTH, T...  1.18 us

profile of v1, /device:TPU:1, one launch (start us, length us, event | category | flops | bytes accessed | tf_op | source)
XLA Modules:
  0.0 56.3 jit_solution(10832761191135515560)
XLA Ops:
  0.0 54.2 %whole.1.logits = f32[2,256,128]{2,1,0:T(8,128)} custom-call(s32[128]{0:T(128)} %readers.1, bf16[3,4,4096]{2,1,0:T(4,128)(2,1)} %bitcast.22, bf16[3,32]{1,0:T(4,128)(2,1)} %head.1, bf16[9,3,32]{2,1,0:T(4,128)(2,1)} %bitcast.23, bf16[27,32,32]{2,1,0:T(8,128)(2,1)} %bitcast.18, bf16[27,32,64]{2,1,0:T(8,128)(2,1)} %bitcast.19, bf16[27,64,64]{2,1,0:T(8,128)(2,1)} %bitcast.13, ...), custom_call_target="tpu_custom_call" | custom-call | flops 10000000000 | bytes 10000000 | tf_op jit(solution)/shard_map/whole/pallas_call | solution.py:745
  54.2 0.0 copy-start
  54.2 0.9 %copy-done = f32[2,256,128]{2,1,0:T(8,128)S(1)} copy-done((f32[2,256,128]{2,1,0:T(8,128)S(1)}, f32[2,256,128]{2,1,0:T(8,128)}, u32[]{:S(2)}) %copy-start) | copy-done | bytes 262168
  55.2 1.2 %finish.1 = f32[3,32,16,32]{3,2,1,0:T(8,128)} custom-call(f32[2,256,128]{2,1,0:T(8,128)S(1)} %copy-done), custom_call_target="tpu_custom_call" | custom-call | tf_op jit(solution)/shard_map/finish/pallas_call | solution.py:792
Async XLA Ops:
  54.2 1.0 %copy-start = (f32[2,256,128]{2,1,0:T(8,128)S(1)}, f32[2,256,128]{2,1,0:T(8,128)}, u32[]{:S(2)}) copy-start(f32[2,256,128]{2,1,0:T(8,128)} %whole.1.logits) | copy-start | bytes 786436

commit v2 on v0

--- a/solution.py
+++ b/solution.py
@@ -382,7 +382,7 @@
     base_ref, z_ref, a_ref,
     quads, skip, in_ref, b_ref, s_ref,
     coarse, middle, ci_ref, co_ref, s2_ref, u1_ref, mi_ref, mm_ref, u2_ref, fi_ref, fm_ref,
-    part_ref, last_ref, first_ref, second_ref, turn_ref, bricks_ref,
+    part_ref, last_ref, bricks_ref,
     load_sems, row_send, row_recv, near_send, near_recv,
     quad_send, quad_recv, skip_send, skip_recv, coarse_send, coarse_recv, middle_send, middle_recv,
 ):
@@ -634,7 +634,7 @@
             tile = jnp.maximum(acc[:, 128 * py : 128 * py + 128], 0.0)
             store_middle(mm_ref, 2 * yg + py, tile, m)
 
-    conv_lines(mi_ref, w_mm, (2, 2, 3), 11, middle_merge, u1_ref)
+    conv_lines(mi_ref, w_mm, (1,) * 7, 11, middle_merge, u1_ref)
     clear_outside(mm_ref, 3, 1, ty, tx, m, split=True)
 
     def middle_final(yg, acc):
@@ -642,7 +642,7 @@
             tile = jnp.maximum(acc[:, 128 * py : 128 * py + 128], 0.0)
             store_single(u2_ref, 2 * yg + py, tile, m)
 
-    conv_lines(mm_ref, w_mf, (2, 2, 2), 10, middle_final)
+    conv_lines(mm_ref, w_mf, (1,) * 6, 10, middle_final)
     clear_outside(u2_ref, 2, 2, ty, tx, m)
 
 
@@ -670,20 +670,19 @@
         w_head[...],
         preferred_element_type=F32,
     )
-    first_ref[...] = logits[:, :128]
-    second_ref[...] = logits[:, 128:]
-
-    def finished(k):
-        turn_ref[k, pl.ds(0, 16, stride=2), :] = first_ref[pl.ds(k, 16, stride=16), :]
-        turn_ref[k, pl.ds(1, 16, stride=2), :] = second_ref[pl.ds(k, 16, stride=16), :]
+    out[0] = logits[:, :128]
+    out[1] = logits[:, 128:]
+
+
+def finish_kernel(logits, out, turn_ref):
+    for k in range(16):
+        turn_ref[k, pl.ds(0, 16, stride=2), :] = logits[0, pl.ds(k, 16, stride=16), :]
+        turn_ref[k, pl.ds(1, 16, stride=2), :] = logits[1, pl.ds(k, 16, stride=16), :]
         turned = turn_ref[k].T
         for c in range(3):
             for pz in range(2):
                 row = 32 * c + 16 * pz
                 out[c, 2 * k + pz] = turned[row : row + 16]
-
-    for k in range(16):
-        finished(k)
 
 
 def per_device(
@@ -727,9 +726,9 @@
     def full(*shape):
         return pltpu.VMEM(shape, F32)
 
-    return pl.pallas_call(
+    logits = pl.pallas_call(
         whole_kernel,
-        out_shape=jax.ShapeDtypeStruct((3, DEPTH, TILE_Y, TILE_X), F32),
+        out_shape=jax.ShapeDtypeStruct((2, 256, 128), F32),
         in_specs=[smem] + [vmem] * 3 + [hbm] * 9,
         out_specs=vmem,
         scratch_shapes=[half(*w.shape) for w in weights]
@@ -760,9 +759,6 @@
             half(18, 17, 16, 256),
             full(9, 272, 256),
             half(8, 256, 256),
-            full(256, 128),
-            full(256, 128),
-            full(16, 32, 128),
             full(3, 128, 128),
             dma((9,)),
             dma((8,)),
@@ -777,6 +773,15 @@
         ),
         cost_estimate=pl.CostEstimate(flops=10**10, bytes_accessed=10**7, transcendentals=0),
     )(stretch_reader, raw_bricks[0], affinity_head, opening, *weights)
+    return pl.pallas_call(
+        finish_kernel,
+        out_shape=jax.ShapeDtypeStruct((3, DEPTH, TILE_Y, TILE_X), F32),
+        in_specs=[vmem],
+        out_specs=vmem,
+        scratch_shapes=[full(16, 32, 128)],
+        name="finish",
+        compiler_params=pltpu.CompilerParams(vmem_limit_bytes=4 * MIB),
+    )(logits)
 
 
 def solution(mesh):

time: 53.5 us -> 52 us (0.972)
  local copies, waits for them, and re-layouts: 2.06 us -> 0.94 us
    unnamed x1 -> x2, local copies, waits for them, and re-layouts: 2.06 us -> 0.94 us
    pallas_call x1 -> x2, Pallas kernels: 51.3 us -> 50.9 us  [the longest x1 49.7 us: per_device(): pl.pallas_call(whole_kernel, out_shape=jax.ShapeDtypeStruct((2, 256, 128)...]
where the time goes in v2:
time: 52 us; the launch traced here: 51.9 us
  Pallas kernels  50.9 us (98%)
  local copies, waits for them, and re-layouts  0.94 us (2%)
    pallas_call x1, Pallas kernels, per_device(): pl.pallas_call(whole_kernel, out_shape=jax.ShapeDtypeStruct((2, 256, 128)...  49.7 us
    pallas_call x1, Pallas kernels, per_device(): pl.pallas_call(finish_kernel, out_shape=jax.ShapeDtypeStruct((3, DEPTH, T...  1.18 us

profile of v2, /device:TPU:1, one launch (start us, length us, event | category | flops | bytes accessed | tf_op | source)
XLA Modules:
  0.0 51.9 jit_solution(8135574364897863059)
XLA Ops:
  0.0 49.7 %whole.1.logits = f32[2,256,128]{2,1,0:T(8,128)} custom-call(s32[128]{0:T(128)} %readers.1, bf16[3,4,4096]{2,1,0:T(4,128)(2,1)} %bitcast.22, bf16[3,32]{1,0:T(4,128)(2,1)} %head.1, bf16[9,3,32]{2,1,0:T(4,128)(2,1)} %bitcast.23, bf16[27,32,32]{2,1,0:T(8,128)(2,1)} %bitcast.18, bf16[27,32,64]{2,1,0:T(8,128)(2,1)} %bitcast.19, bf16[27,64,64]{2,1,0:T(8,128)(2,1)} %bitcast.13, ...), custom_call_target="tpu_custom_call" | custom-call | flops 10000000000 | bytes 10000000 | tf_op jit(solution)/shard_map/whole/pallas_call | solution.py:729
  49.7 0.0 copy-start
  49.8 0.9 %copy-done = f32[2,256,128]{2,1,0:T(8,128)S(1)} copy-done((f32[2,256,128]{2,1,0:T(8,128)S(1)}, f32[2,256,128]{2,1,0:T(8,128)}, u32[]{:S(2)}) %copy-start) | copy-done | bytes 262168
  50.7 1.2 %finish.1 = f32[3,32,16,32]{3,2,1,0:T(8,128)} custom-call(f32[2,256,128]{2,1,0:T(8,128)S(1)} %copy-done), custom_call_target="tpu_custom_call" | custom-call | tf_op jit(solution)/shard_map/finish/pallas_call | solution.py:776
Async XLA Ops:
  49.7 1.0 %copy-start = (f32[2,256,128]{2,1,0:T(8,128)S(1)}, f32[2,256,128]{2,1,0:T(8,128)}, u32[]{:S(2)}) copy-start(f32[2,256,128]{2,1,0:T(8,128)} %whole.1.logits) | copy-start | bytes 786436

commit v3 on v2

--- a/solution.py
+++ b/solution.py
@@ -585,7 +585,7 @@
         x = as_rows(skip[y]).astype(F32)
         store_fine(fi_ref, y, x, m)
 
-    loop(20, fine_in, 2)
+    loop(20, fine_in, 4)
     for yg in range(9):
         part_ref[yg] = jnp.dot(
             window(fi_ref, yg, 17), w_fm[0:2048], preferred_element_type=F32
@@ -599,7 +599,7 @@
         x = as_rows(jnp.concatenate([x, jnp.zeros_like(x)], axis=1))
         store_middle(ci_ref, y, x, m)
 
-    loop(12, coarse_in)
+    loop(12, coarse_in, 4)
 
     def coarse_open(yg, acc):
         for py in range(2):
@@ -627,7 +627,7 @@
         x = as_rows(middle[y]).astype(F32)
         store_middle(mi_ref, y, x, m)
 
-    loop(16, middle_in)
+    loop(16, middle_in, 4)
 
     def middle_merge(yg, acc):
         for py in range(2):

time: 52 us -> 51.9 us (level)
  no operation moved by 1% of the time
where the time goes in v3:
time: 51.9 us; the launch traced here: 51.7 us
  Pallas kernels  50.7 us (98%)
  local copies, waits for them, and re-layouts  0.94 us (2%)
    pallas_call x1, Pallas kernels, per_device(): pl.pallas_call(whole_kernel, out_shape=jax.ShapeDtypeStruct((2, 256, 128)...  49.6 us
    pallas_call x1, Pallas kernels, per_device(): pl.pallas_call(finish_kernel, out_shape=jax.ShapeDtypeStruct((3, DEPTH, T...  1.18 us

profile of v3, /device:TPU:1, one launch (start us, length us, event | category | flops | bytes accessed | tf_op | source)
XLA Modules:
  0.0 51.7 jit_solution(1073277054983695666)
XLA Ops:
  0.0 49.6 %whole.1.logits = f32[2,256,128]{2,1,0:T(8,128)} custom-call(s32[128]{0:T(128)} %readers.1, bf16[3,4,4096]{2,1,0:T(4,128)(2,1)} %bitcast.22, bf16[3,32]{1,0:T(4,128)(2,1)} %head.1, bf16[9,3,32]{2,1,0:T(4,128)(2,1)} %bitcast.23, bf16[27,32,32]{2,1,0:T(8,128)(2,1)} %bitcast.18, bf16[27,32,64]{2,1,0:T(8,128)(2,1)} %bitcast.19, bf16[27,64,64]{2,1,0:T(8,128)(2,1)} %bitcast.13, ...), custom_call_target="tpu_custom_call" | custom-call | flops 10000000000 | bytes 10000000 | tf_op jit(solution)/shard_map/whole/pallas_call | solution.py:729
  49.6 0.0 copy-start
  49.6 0.9 %copy-done = f32[2,256,128]{2,1,0:T(8,128)S(1)} copy-done((f32[2,256,128]{2,1,0:T(8,128)S(1)}, f32[2,256,128]{2,1,0:T(8,128)}, u32[]{:S(2)}) %copy-start) | copy-done | bytes 262168
  50.5 1.2 %finish.1 = f32[3,32,16,32]{3,2,1,0:T(8,128)} custom-call(f32[2,256,128]{2,1,0:T(8,128)S(1)} %copy-done), custom_call_target="tpu_custom_call" | custom-call | tf_op jit(solution)/shard_map/finish/pallas_call | solution.py:776
Async XLA Ops:
  49.6 1.0 %copy-start = (f32[2,256,128]{2,1,0:T(8,128)S(1)}, f32[2,256,128]{2,1,0:T(8,128)}, u32[]{:S(2)}) copy-start(f32[2,256,128]{2,1,0:T(8,128)} %whole.1.logits) | copy-start | bytes 786436
